TPU v7x, 32 devices: a whole 2x2x4 slice. The times are simulated.
32 devices in a mesh: ens: 1, wide: 16 (over z, y, x), lev: 2 (over core).
Axes of the slice: x: 2, y: 2, z: 4, core: 2. Of those that a mesh axis runs over, the one named last changes fastest.
Arguments:
- model_state: float32 [4, 8, 128, 1024], P('ens', 'lev', 'wide'), may hold values from -6 to 6
- grid_points: int32 [128], P('wide'), may hold values from 32 to 1024, as said below
- quad_weights: float32 [128], P('wide'), may hold values from 0.5 to 2
- slot_waves: int32 [512], replicated, may hold values from 0 to 511, each once
- legendre: bfloat16 [512, 512, 128], P(('wide', 'lev')), may hold values from -0.5 to 0.5
- mode_in: float32 [8, 8], replicated, may hold values from -2 to 2
- mode_out: float32 [8, 8], replicated, may hold values from -2 to 2
- mode_rates: float32 [8], replicated, may hold values from 0.05 to 2
Outputs:
- new_state: float32 [4, 8, 128, 1024], P('ens', 'lev', 'wide')
- energy: float32 [8, 512], P('ens', ('wide', 'lev'))
Inputs may be any that keep to these rules, and one draw needn't show every extreme that they name: `slot_waves`: each wavenumber is held by exactly one slot. `grid_points`: the two latitudes next to the equator have 1024 points.
All inputs are finite; a program needn't handle non-finite values.
Results may differ from a plain program's by a relative error of at most 0.0067.
Values may be sent and summed in bfloat16 or wider, within the bound.
A program may use at most 64 MiB of HBM per device.

v0:
```python
from functools import partial
import math

import jax
import jax.numpy as jnp
from jax import lax
from jax.sharding import PartitionSpec as P


def tendency(fields):
    diverge = fields[0]
    first = diverge - 0.25 * diverge * diverge
    others = fields[1:] - 0.25 * fields[1:] * diverge[None]
    return jnp.concatenate([first[None], others], axis=0)


def harmonic_tables(points, longitudes, wave_count, modes_axis):
    layout = (longitudes, wave_count) if modes_axis == 1 else (wave_count, longitudes)
    position = lax.broadcasted_iota(jnp.int32, layout, 1 - modes_axis)
    wavenum = lax.broadcasted_iota(jnp.int32, layout, modes_axis)
    phases = wavenum * position % points
    angles = phases.astype(jnp.float32) * (2.0 * math.pi / points.astype(jnp.float32))
    inside = (position < points) & (wavenum < (points + 1) // 2)
    cosine_part = jnp.where(inside, jnp.cos(angles), 0.0)
    sine_part = jnp.where(inside, jnp.sin(angles), 0.0)
    return (cosine_part, sine_part, wavenum)


def forward_lat(longitudes, wave_count, element):
    lat_block, points, weight = element
    cosine_part, sine_part, wavenum = harmonic_tables(points, longitudes, wave_count, 1)
    tables = jnp.concatenate([cosine_part, -sine_part], axis=1).astype(jnp.bfloat16)
    row_block = lat_block.reshape(-1, longitudes)
    fourier = jnp.dot(row_block, tables, preferred_element_type=jnp.float32)
    weighting = weight / points.astype(jnp.float32)
    return (
        (fourier * weighting)
        .astype(jnp.bfloat16)
        .reshape(lat_block.shape[0], lat_block.shape[1], 2, wave_count)
    )


def inverse_lat(longitudes, wave_count, element):
    coefficients, points = element
    cosine_part, sine_part, wavenum = harmonic_tables(points, longitudes, wave_count, 0)
    factor = jnp.where(wavenum == 0, 1.0, 2.0)
    tables = jnp.concatenate([factor * cosine_part, -factor * sine_part], axis=0).astype(
        jnp.bfloat16
    )
    values = jnp.dot(
        coefficients.reshape(-1, 2 * wave_count), tables, preferred_element_type=jnp.float32
    )
    return tendency(values.reshape(coefficients.shape[0], coefficients.shape[1], longitudes))


def implicit_step(spectral, mode_in, mode_out, mode_rates, levels, fields_count):
    slot_count, wave_count = (spectral.shape[0], spectral.shape[1])
    blocks = spectral.reshape(slot_count, wave_count, levels, fields_count, 2)
    degree = jnp.arange(wave_count, dtype=jnp.float32)
    laplace = degree * (degree + 1.0) / (wave_count * wave_count)
    laplace_four = laplace[None, :, None, None]
    highest = lax.Precision.HIGHEST
    diverge = blocks[:, :, :, 0, :]
    geopot = blocks[:, :, :, 1, :]
    tracer = blocks[:, :, :, 2:, :]
    div_modes = jnp.einsum("kl,snlc->snkc", mode_in, diverge, precision=highest)
    geo_modes = jnp.einsum("kl,snlc->snkc", mode_in, geopot, precision=highest)
    rate_grid = mode_rates[None, None, :, None]
    div_next = (div_modes + 2.0 * laplace_four * geo_modes) / (1.0 + 4.0 * laplace_four * rate_grid)
    geo_next = geo_modes - 2.0 * rate_grid * div_next
    div_level = jnp.einsum("lk,snkc->snlc", mode_out, div_next, precision=highest)
    geo_level = jnp.einsum("lk,snkc->snlc", mode_out, geo_next, precision=highest)
    tracer_next = tracer / (1.0 + 8.0 * laplace * laplace)[None, :, None, None, None]
    updated = jnp.concatenate(
        [div_level[:, :, :, None, :], geo_level[:, :, :, None, :], tracer_next], axis=3
    )
    energy = (
        jnp.einsum("snlc,snlc->ln", div_level, div_level, precision=highest)
        * (wave_count / (degree + 1.0))[None, :]
    )
    return (updated.reshape(slot_count, wave_count, -1), energy)


def body(
    model_state, grid_points, quad_weights, slot_waves, legendre, mode_in, mode_out, mode_rates
):
    fields_count, lev_local, lat_local, longitudes = model_state.shape
    slot_count, wave_count, lat_all = legendre.shape
    levels = mode_in.shape[0]
    components = fields_count * 2
    wide_size = lax.axis_size("wide")
    lev_size = lax.axis_size("lev")
    explicit = tendency(model_state).astype(jnp.bfloat16)
    by_lat = jnp.transpose(explicit, (2, 0, 1, 3))
    fourier = lax.map(
        partial(forward_lat, longitudes, wave_count), (by_lat, grid_points, quad_weights)
    )
    ordered = jnp.take(fourier, slot_waves, axis=4)
    ordered = jnp.transpose(ordered, (4, 2, 1, 3, 0)).reshape(
        wave_count, lev_local, components, lat_local
    )
    outgoing = ordered.reshape(wave_count, 1, lev_local, components, lat_local)
    received = lax.all_to_all(outgoing, ("wide", "lev"), split_axis=0, concat_axis=1, tiled=True)
    received = received.reshape(slot_count, wide_size, lev_size, lev_local, components, lat_local)
    wave_rows = jnp.transpose(received, (0, 2, 3, 4, 1, 5)).reshape(
        slot_count, levels * components, lat_all
    )
    device = lax.axis_index("wide") * lev_size + lax.axis_index("lev")
    own_waves = lax.dynamic_slice_in_dim(slot_waves, device * slot_count, slot_count)
    degree = lax.broadcasted_iota(jnp.int32, (slot_count, wave_count, 1), 1)
    spectral = jnp.einsum("snj,scj->snc", legendre, wave_rows, preferred_element_type=jnp.float32)
    spectral = jnp.where(degree >= own_waves[:, None, None], spectral, 0.0)
    updated, energy_term = implicit_step(
        spectral, mode_in, mode_out, mode_rates, levels, fields_count
    )
    energy = lax.psum_scatter(energy_term, ("wide", "lev"), scatter_dimension=1, tiled=True)
    packed = updated.astype(jnp.bfloat16)
    returned = jnp.einsum("snc,snj->scj", packed, legendre, preferred_element_type=jnp.float32)
    returned = returned.astype(jnp.bfloat16).reshape(slot_count, levels, components, lat_all)
    slot_of = (
        jnp.zeros((wave_count,), jnp.int32).at[slot_waves].set(lax.iota(jnp.int32, wave_count))
    )
    arranged = returned.reshape(slot_count, lev_size, lev_local, components, wide_size, lat_local)
    arranged = jnp.transpose(arranged, (4, 1, 0, 2, 3, 5)).reshape(
        wide_size * lev_size, 1, slot_count, lev_local, components, lat_local
    )
    arrived = lax.all_to_all(arranged, ("wide", "lev"), split_axis=0, concat_axis=1, tiled=True)
    arrived = arrived.reshape(wave_count, lev_local, components, lat_local)
    by_wave = jnp.take(arrived, slot_of, axis=0)
    by_wave = by_wave.reshape(wave_count, lev_local, fields_count, 2, lat_local).transpose(
        4, 2, 1, 3, 0
    )
    gridded = lax.map(partial(inverse_lat, longitudes, wave_count), (by_wave, grid_points))
    new_state = jnp.transpose(gridded, (1, 2, 0, 3))
    return (new_state, energy)


def solution(mesh):
    return jax.shard_map(
        body,
        mesh=mesh,
        in_specs=(
            P("ens", "lev", "wide", None),
            P("wide"),
            P("wide"),
            P(),
            P(("wide", "lev"), None, None),
            P(),
            P(),
            P(),
        ),
        out_specs=(P("ens", "lev", "wide", None), P("ens", ("wide", "lev"))),
        check_vma=False,
    )
```

profile of v0, /device:TPU:0, one launch (start us, length us, event | category | flops | bytes accessed | tf_op | source)
XLA Modules:
  0.0 860.0 jit_solution(14757606000627807612)
XLA Ops:
  11.3 296.7 %while.24 = (s32[]{:T(128)}, bf16[8,4,4,2,512]{4,3,2,1,0:T(2,128)(2,1)}, bf16[8,4,4,1024]{3,2,1,0:T(4,128)(2,1)S(1)}, s32[8]{0:T(128)S(1)}, f32[8]{0:T(128)S(1)}...) while((s32[]{:T(128)}, bf16[8,4,4,2,512]{4,3,2,1,0:T(2,128)(2,1)}, bf16[8,4,4,1024]{3,2,1,0:T(4,128)(2,1)S(1)}, ...), condition=%wide.region_2.3_spmd, body=%wide.region_1.2_spmd.sunk | while | flops 46171672 | bytes 4525935 | solution.py:95
  15.2 29.6 %fusion.83 = (bf16[1024,512]{1,0:T(8,128)(2,1)S(1)}, bf16[1024,512]{1,0:T(8,128)(2,1)}) fusion(f32[]{:T(128)S(6)} %div.94, s32[]{:T(128)S(6)} %select_n.179, pred[]{:T(512)S(6)} %lt.148, pred[512]{0:T(512)(128)(4,1)S(1)} %iota_compare_fusion.10, pred[1024]{0:T(1024)(128)(4,1)S(1)} %iota_compare_fusion.11), kind=kLoop, calls=%fused_computation.6.clone.1 | loop fusion | flops 8388608 | bytes 2098697 | tf_op jit(solution)/shard_map/convert
  52.2 29.6 %fusion.83 = (bf16[1024,512]{1,0:T(8,128)(2,1)S(1)}, bf16[1024,512]{1,0:T(8,128)(2,1)}) fusion(f32[]{:T(128)S(6)} %div.94, s32[]{:T(128)S(6)} %select_n.179, pred[]{:T(512)S(6)} %lt.148, pred[512]{0:T(512)(128)(4,1)S(1)} %iota_compare_fusion.10, pred[1024]{0:T(1024)(128)(4,1)S(1)} %iota_compare_fusion.11), kind=kLoop, calls=%fused_computation.6.clone.1 | loop fusion | flops 8388608 | bytes 2098697 | tf_op jit(solution)/shard_map/convert
  89.3 29.6 %fusion.83 = (bf16[1024,512]{1,0:T(8,128)(2,1)S(1)}, bf16[1024,512]{1,0:T(8,128)(2,1)}) fusion(f32[]{:T(128)S(6)} %div.94, s32[]{:T(128)S(6)} %select_n.179, pred[]{:T(512)S(6)} %lt.148, pred[512]{0:T(512)(128)(4,1)S(1)} %iota_compare_fusion.10, pred[1024]{0:T(1024)(128)(4,1)S(1)} %iota_compare_fusion.11), kind=kLoop, calls=%fused_computation.6.clone.1 | loop fusion | flops 8388608 | bytes 2098697 | tf_op jit(solution)/shard_map/convert
  126.4 29.6 %fusion.83 = (bf16[1024,512]{1,0:T(8,128)(2,1)S(1)}, bf16[1024,512]{1,0:T(8,128)(2,1)}) fusion(f32[]{:T(128)S(6)} %div.94, s32[]{:T(128)S(6)} %select_n.179, pred[]{:T(512)S(6)} %lt.148, pred[512]{0:T(512)(128)(4,1)S(1)} %iota_compare_fusion.10, pred[1024]{0:T(1024)(128)(4,1)S(1)} %iota_compare_fusion.11), kind=kLoop, calls=%fused_computation.6.clone.1 | loop fusion | flops 8388608 | bytes 2098697 | tf_op jit(solution)/shard_map/convert
  163.5 29.6 %fusion.83 = (bf16[1024,512]{1,0:T(8,128)(2,1)S(1)}, bf16[1024,512]{1,0:T(8,128)(2,1)}) fusion(f32[]{:T(128)S(6)} %div.94, s32[]{:T(128)S(6)} %select_n.179, pred[]{:T(512)S(6)} %lt.148, pred[512]{0:T(512)(128)(4,1)S(1)} %iota_compare_fusion.10, pred[1024]{0:T(1024)(128)(4,1)S(1)} %iota_compare_fusion.11), kind=kLoop, calls=%fused_computation.6.clone.1 | loop fusion | flops 8388608 | bytes 2098697 | tf_op jit(solution)/shard_map/convert
  200.6 29.6 %fusion.83 = (bf16[1024,512]{1,0:T(8,128)(2,1)S(1)}, bf16[1024,512]{1,0:T(8,128)(2,1)}) fusion(f32[]{:T(128)S(6)} %div.94, s32[]{:T(128)S(6)} %select_n.179, pred[]{:T(512)S(6)} %lt.148, pred[512]{0:T(512)(128)(4,1)S(1)} %iota_compare_fusion.10, pred[1024]{0:T(1024)(128)(4,1)S(1)} %iota_compare_fusion.11), kind=kLoop, calls=%fused_computation.6.clone.1 | loop fusion | flops 8388608 | bytes 2098697 | tf_op jit(solution)/shard_map/convert
  237.6 29.6 %fusion.83 = (bf16[1024,512]{1,0:T(8,128)(2,1)S(1)}, bf16[1024,512]{1,0:T(8,128)(2,1)}) fusion(f32[]{:T(128)S(6)} %div.94, s32[]{:T(128)S(6)} %select_n.179, pred[]{:T(512)S(6)} %lt.148, pred[512]{0:T(512)(128)(4,1)S(1)} %iota_compare_fusion.10, pred[1024]{0:T(1024)(128)(4,1)S(1)} %iota_compare_fusion.11), kind=kLoop, calls=%fused_computation.6.clone.1 | loop fusion | flops 8388608 | bytes 2098697 | tf_op jit(solution)/shard_map/convert
  274.7 29.6 %fusion.83 = (bf16[1024,512]{1,0:T(8,128)(2,1)S(1)}, bf16[1024,512]{1,0:T(8,128)(2,1)}) fusion(f32[]{:T(128)S(6)} %div.94, s32[]{:T(128)S(6)} %select_n.179, pred[]{:T(512)S(6)} %lt.148, pred[512]{0:T(512)(128)(4,1)S(1)} %iota_compare_fusion.10, pred[1024]{0:T(1024)(128)(4,1)S(1)} %iota_compare_fusion.11), kind=kLoop, calls=%fused_computation.6.clone.1 | loop fusion | flops 8388608 | bytes 2098697 | tf_op jit(solution)/shard_map/convert
  307.9 6.4 copy.52
  314.3 27.8 %gather_fusion = bf16[512,8,4,4,2]{1,3,4,2,0:T(4,128)(2,1)} fusion(bf16[8,4,4,2,512]{0,2,4,3,1:T(4,128)(2,1)} %copy.52, s32[1024]{0:T(1024)S(1)} %pad_clamp_fusion.1), kind=kCustom, calls=%fused_computation | custom fusion | bytes 526336 | tf_op jit(solution)/shard_map/jit(_take)/gather | solution.py:98
  342.1 4.7 broadcast_select_fusion
  349.5 6.5 reshape.192
  356.0 7.3 all-to-all-start
  366.7 7.2 all-to-all-done
  373.9 6.0 reshape.193
  379.8 7.0 copy.80
  410.2 3.5 copy.64
  413.8 4.6 reshape.194
  421.9 137.2 %reduce-scatter.4.cloned.1.call-done = f32[16,8]{1,0:T(8,128)} async-done(((f32[512,8]{1,0:T(8,128)}), f32[16,8]{1,0:T(8,128)}) %reduce-scatter.4.cloned.1.call-update) | async-done | bytes 528
  562.9 7.9 copy.81
  570.8 5.4 gather_fusion.1
  576.2 4.4 copy.68
  580.9 271.1 %while.25 = (s32[]{:T(128)}, f32[8,4,4,1024]{3,0,2,1:T(8,128)S(1)}, bf16[8,4,4,2,512]{4,3,2,1,0:T(2,128)(2,1)S(1)}, s32[8]{0:T(128)S(1)}, s32[]{:T(128)}, /*index=5*/f32[]{:T(128)}, s32[]{:T(128)}, s32[]{:T(128)}) while((s32[]{:T(128)}, f32[8,4,4,1024]{3,0,2,1:T(8,128)S(1)}, bf16[8,4,4,2,512]{4,3,2,1,0:T(2,128)(2,1)S(1)}, s32[8]{0:T(128)S(1)}, ...), condition=%wide.region_4.5_spmd, body=%wide.region_3.4_spmd.sunk | while | flops 46717976 | bytes 5188943 | solution.py:133
  584.8 28.9 %fusion.88 = (bf16[512,1024]{1,0:T(8,128)(2,1)S(1)}, bf16[512,1024]{1,0:T(8,128)(2,1)S(1)}) fusion(f32[]{:T(128)S(6)} %div.99, s32[]{:T(128)S(6)} %select_n.184, f32[512]{0:T(512)S(1)} %get-tuple-element.236, pred[]{:T(512)S(6)} %lt.154, pred[1024]{0:T(1024)(128)(4,1)S(1)} %iota_compare_fusion.12, pred[512]{0:T(512)(128)(4,1)S(1)} %iota_compare_fusion.13, ...), kind=kLoop, calls=%fused_computation.31.clone.1 | loop fusion | flops 8912896 | bytes 2102793 | tf_op jit(solution)/shard_map/convert.2
  618.7 28.9 %fusion.88 = (bf16[512,1024]{1,0:T(8,128)(2,1)S(1)}, bf16[512,1024]{1,0:T(8,128)(2,1)S(1)}) fusion(f32[]{:T(128)S(6)} %div.99, s32[]{:T(128)S(6)} %select_n.184, f32[512]{0:T(512)S(1)} %get-tuple-element.236, pred[]{:T(512)S(6)} %lt.154, pred[1024]{0:T(1024)(128)(4,1)S(1)} %iota_compare_fusion.12, pred[512]{0:T(512)(128)(4,1)S(1)} %iota_compare_fusion.13, ...), kind=kLoop, calls=%fused_computation.31.clone.1 | loop fusion | flops 8912896 | bytes 2102793 | tf_op jit(solution)/shard_map/convert.2
  652.6 28.9 %fusion.88 = (bf16[512,1024]{1,0:T(8,128)(2,1)S(1)}, bf16[512,1024]{1,0:T(8,128)(2,1)S(1)}) fusion(f32[]{:T(128)S(6)} %div.99, s32[]{:T(128)S(6)} %select_n.184, f32[512]{0:T(512)S(1)} %get-tuple-element.236, pred[]{:T(512)S(6)} %lt.154, pred[1024]{0:T(1024)(128)(4,1)S(1)} %iota_compare_fusion.12, pred[512]{0:T(512)(128)(4,1)S(1)} %iota_compare_fusion.13, ...), kind=kLoop, calls=%fused_computation.31.clone.1 | loop fusion | flops 8912896 | bytes 2102793 | tf_op jit(solution)/shard_map/convert.2
  686.5 28.9 %fusion.88 = (bf16[512,1024]{1,0:T(8,128)(2,1)S(1)}, bf16[512,1024]{1,0:T(8,128)(2,1)S(1)}) fusion(f32[]{:T(128)S(6)} %div.99, s32[]{:T(128)S(6)} %select_n.184, f32[512]{0:T(512)S(1)} %get-tuple-element.236, pred[]{:T(512)S(6)} %lt.154, pred[1024]{0:T(1024)(128)(4,1)S(1)} %iota_compare_fusion.12, pred[512]{0:T(512)(128)(4,1)S(1)} %iota_compare_fusion.13, ...), kind=kLoop, calls=%fused_computation.31.clone.1 | loop fusion | flops 8912896 | bytes 2102793 | tf_op jit(solution)/shard_map/convert.2
  720.3 28.9 %fusion.88 = (bf16[512,1024]{1,0:T(8,128)(2,1)S(1)}, bf16[512,1024]{1,0:T(8,128)(2,1)S(1)}) fusion(f32[]{:T(128)S(6)} %div.99, s32[]{:T(128)S(6)} %select_n.184, f32[512]{0:T(512)S(1)} %get-tuple-element.236, pred[]{:T(512)S(6)} %lt.154, pred[1024]{0:T(1024)(128)(4,1)S(1)} %iota_compare_fusion.12, pred[512]{0:T(512)(128)(4,1)S(1)} %iota_compare_fusion.13, ...), kind=kLoop, calls=%fused_computation.31.clone.1 | loop fusion | flops 8912896 | bytes 2102793 | tf_op jit(solution)/shard_map/convert.2
  754.2 28.9 %fusion.88 = (bf16[512,1024]{1,0:T(8,128)(2,1)S(1)}, bf16[512,1024]{1,0:T(8,128)(2,1)S(1)}) fusion(f32[]{:T(128)S(6)} %div.99, s32[]{:T(128)S(6)} %select_n.184, f32[512]{0:T(512)S(1)} %get-tuple-element.236, pred[]{:T(512)S(6)} %lt.154, pred[1024]{0:T(1024)(128)(4,1)S(1)} %iota_compare_fusion.12, pred[512]{0:T(512)(128)(4,1)S(1)} %iota_compare_fusion.13, ...), kind=kLoop, calls=%fused_computation.31.clone.1 | loop fusion | flops 8912896 | bytes 2102793 | tf_op jit(solution)/shard_map/convert.2
  788.1 28.9 %fusion.88 = (bf16[512,1024]{1,0:T(8,128)(2,1)S(1)}, bf16[512,1024]{1,0:T(8,128)(2,1)S(1)}) fusion(f32[]{:T(128)S(6)} %div.99, s32[]{:T(128)S(6)} %select_n.184, f32[512]{0:T(512)S(1)} %get-tuple-element.236, pred[]{:T(512)S(6)} %lt.154, pred[1024]{0:T(1024)(128)(4,1)S(1)} %iota_compare_fusion.12, pred[512]{0:T(512)(128)(4,1)S(1)} %iota_compare_fusion.13, ...), kind=kLoop, calls=%fused_computation.31.clone.1 | loop fusion | flops 8912896 | bytes 2102793 | tf_op jit(solution)/shard_map/convert.2
  822.0 28.9 %fusion.88 = (bf16[512,1024]{1,0:T(8,128)(2,1)S(1)}, bf16[512,1024]{1,0:T(8,128)(2,1)S(1)}) fusion(f32[]{:T(128)S(6)} %div.99, s32[]{:T(128)S(6)} %select_n.184, f32[512]{0:T(512)S(1)} %get-tuple-element.236, pred[]{:T(512)S(6)} %lt.154, pred[1024]{0:T(1024)(128)(4,1)S(1)} %iota_compare_fusion.12, pred[512]{0:T(512)(128)(4,1)S(1)} %iota_compare_fusion.13, ...), kind=kLoop, calls=%fused_computation.31.clone.1 | loop fusion | flops 8912896 | bytes 2102793 | tf_op jit(solution)/shard_map/convert.2
  (252 shorter events, 93.0 us)
Async XLA Ops:
  7.2 386.0 %copy-start = (bf16[16,512,128]{2,1,0:T(8,128)(2,1)S(1)}, bf16[16,512,128]{2,1,0:T(8,128)(2,1)}, u32[]{:S(2)}) copy-start(bf16[16,512,128]{2,1,0:T(8,128)(2,1)} %param.16) | copy-start | bytes 6291460
  7.2 4.1 copy-start.7
  7.2 4.1 copy-start.6
  349.5 14.6 %copy-start.4 = (f32[8]{0:T(128)S(1)}, f32[8]{0:T(128)}, u32[]{:S(2)}) copy-start(f32[8]{0:T(128)} %param.19) | copy-start | bytes 100
  356.0 17.9 %all-to-all-start = ((bf16[32,2,2048]{2,1,0:T(2,128)(2,1)}), bf16[32,2,2048]{2,1,0:T(2,128)(2,1)S(1)}, u32[]{:S(2)}, u32[]{:S(2)}) async-start(bf16[32,2,2048]{2,1,0:T(2,128)(2,1)} %reshape.192), calls=%async_computation | async-start | bytes 524288 | tf_op jit(solution)/shard_map/all_to_all | solution.py:103
  398.8 1.6 copy-start.3
  400.4 1.3 copy-start.2
  401.7 1.8 copy-start.1
  418.4 142.1 %all-to-all-start.1 = ((bf16[32,2,2048]{2,1,0:T(2,128)(2,1)}), bf16[32,2,2048]{2,1,0:T(2,128)(2,1)S(1)}, u32[]{:S(2)}, u32[]{:S(2)}) async-start(bf16[32,2,2048]{2,1,0:T(2,128)(2,1)} %reshape.194), calls=%async_computation.1 | async-start | bytes 524288 | tf_op jit(solution)/shard_map/all_to_all | solution.py:127
  421.0 138.2 %reduce-scatter.4.cloned.1.call-start = ((), (), s32[]{:S(2)}) async-start(), calls=%async_computation.3 | async-start | bytes 270336
  852.0 0.8 copy-start.5
Sparse Core Ops, SparseCore 0:
  424.1 135.0 reduce-scatter.3
where the time goes:
time: 867 us; the launch traced here: 860 us
  other arithmetic  488 us (56%)
  waiting for transfers between devices  144 us (17%)
  local copies, waits for them, and re-layouts  132 us (15%)
  loops' own time  48.5 us (6%)
  matrix products  22.4 us (3%)
  between operations  14.8 us (2%)
  starting transfers between devices  9.92 us (1%)
    another operation x19, other arithmetic  469 us
    unnamed x2, waiting for transfers between devices  137 us
    gather x1, local copies, waits for them, and re-layouts, body(): ordered = jnp.take(fourier, slot_waves, axis=4)  27.8 us
    another operation x1, loops' own time, body(): lax.map(partial(forward_lat, longitudes, wave_count), (by_lat, grid_point...  26.3 us
    unnamed x22, local copies, waits for them, and re-layouts  22.5 us
    another operation x1, loops' own time, body(): lax.map(partial(inverse_lat, longitudes, wave_count), (by_wave, grid_poin...  22.2 us
  transfers between devices with their start and end apart: 3, of which 2 were waited for; matrix products, arithmetic and copies ran while one was open for 1% of the time, Pallas kernels for 0%

commit v1 on v0

v1 whole, which is shorter than its diff:
```python
from functools import partial
import math

import jax
import jax.numpy as jnp
from jax import lax
from jax.experimental import pallas as pl
from jax.experimental.pallas import tpu as pltpu
from jax.sharding import PartitionSpec as P

LANES = 128
PAD_SLOTS = 16
LATS = 8
VMEM = 40 * 1024 * 1024


def exchange(arrays, stride):
    lane = lax.broadcasted_iota(jnp.int32, arrays[0].shape, 1)
    arrays = list(arrays)
    step = 1
    while step < len(arrays):
        shift = step * stride
        upper = (lane & shift) != 0
        for low in range(len(arrays)):
            if low & step:
                continue
            first, second = arrays[low], arrays[low | step]
            arrays[low] = jnp.where(upper, pltpu.roll(second, shift, 1), first)
            arrays[low | step] = jnp.where(upper, second, pltpu.roll(first, LANES - shift, 1))
        step *= 2
    return arrays


def turn_pair(product, points, inverse):
    turns = jnp.floor(product * inverse + 0.5)
    half = (product - turns * points) * inverse * math.pi
    square = half * half
    cosine = 1.0 / 479001600.0
    for term in (-1.0 / 3628800.0, 1.0 / 40320.0, -1.0 / 720.0, 1.0 / 24.0, -0.5, 1.0):
        cosine = cosine * square + term
    sine = 1.0 / 6227020800.0
    for term in (-1.0 / 39916800.0, 1.0 / 362880.0, -1.0 / 5040.0, 1.0 / 120.0, -1.0 / 6.0, 1.0):
        sine = sine * square + term
    sine = sine * half
    return (1.0 - 2.0 * sine * sine, 2.0 * sine * cosine)


def fill_tables(points, inverse, cos_ref, sin_ref, base_ref):
    rows, lanes = cos_ref.shape
    highs = rows // 16
    row = lax.broadcasted_iota(jnp.int32, (16 + highs, lanes), 0)
    lane = lax.broadcasted_iota(jnp.int32, (16 + highs, lanes), 1)
    number = jnp.where(row < 16, row, (row - 16) * 16)
    cosine, sine = turn_pair((number * lane).astype(jnp.float32), points, inverse)
    base_ref[0] = cosine
    base_ref[1] = sine
    width = 256
    for start in range(0, lanes, width):
        cut = pl.ds(start, width)
        low_cos = base_ref[0, 0:16, cut]
        low_sin = base_ref[1, 0:16, cut]
        for high in range(highs):
            high_cos = base_ref[0, 16 + high : 17 + high, cut]
            high_sin = base_ref[1, 16 + high : 17 + high, cut]
            place = pl.ds(high * 16, 16)
            cos_ref[place, cut] = (high_cos * low_cos - high_sin * low_sin).astype(jnp.bfloat16)
            sin_ref[place, cut] = (high_sin * low_cos + high_cos * low_sin).astype(jnp.bfloat16)


def strided_rows(ref, start, count, stride):
    place = pl.ds(start, count, stride=stride) if stride else slice(None)
    return jnp.concatenate([ref[block, place, :] for block in range(ref.shape[0])], axis=1)


def store_strided(ref, start, count, stride, value):
    place = pl.ds(start, count, stride=stride)
    for block in range(ref.shape[0]):
        ref[block, place, :] = value[:, block * LANES : (block + 1) * LANES]


def tendency_tile(read, write, rows, fields):
    for start in range(0, rows // fields, 8):
        diverge = read(pl.ds(start, 8))
        for field in range(fields):
            place = pl.ds(field * (rows // fields) + start, 8)
            value = read(place)
            write(place, value - 0.25 * value * diverge)


def tendency_in(source, target, fields):
    for block in range(target.shape[0]):
        cut = pl.ds(block * LANES, LANES)

        def write(place, value):
            target[block, place, :] = value

        tendency_tile(lambda place: source[place, cut], write, source.shape[0], fields)


def tendency_out(source, target, fields):
    for block in range(source.shape[0]):
        cut = pl.ds(block * LANES, LANES)

        def write(place, value):
            target[place, cut] = value

        tendency_tile(lambda place: source[block, place, :], write, target.shape[0], fields)


def select_matrix(waves, wave_count):
    row = lax.broadcasted_iota(jnp.int32, (wave_count, waves.shape[1]), 0)
    return jnp.where(row == waves, 1.0, 0.0).astype(jnp.bfloat16)


def forward_kernel(
    fields, wave_count, points_ref, weight_ref, state_ref, waves_ref, out_ref,
    explicit, cos_ref, sin_ref, base_ref, rows_ref, moved,
):
    longitudes = state_ref.shape[1]
    series = state_ref.shape[0] // LATS
    comps = 2 * series
    tendency_in(state_ref, explicit, fields)
    position = lax.broadcasted_iota(jnp.int32, (series, longitudes), 1)
    wave = lax.broadcasted_iota(jnp.int32, (series, wave_count), 1)

    def one_lat(lat, carry):
        points = points_ref[lat]
        count = points.astype(jnp.float32)
        inverse = 1.0 / jnp.full((1, wave_count), count, jnp.float32)
        fill_tables(count, inverse, cos_ref, sin_ref, base_ref)
        data = strided_rows(explicit, lat, series, LATS)
        data = jnp.where(position < points, data, 0.0).astype(jnp.bfloat16)
        scale = jnp.where(wave < (points + 1) // 2, inverse * weight_ref[lat], 0.0)
        first = jnp.dot(data, cos_ref[...], preferred_element_type=jnp.float32)
        second = jnp.dot(data, sin_ref[...], preferred_element_type=jnp.float32)
        start = lat * comps
        store_strided(rows_ref, start, series, 2, first * scale)
        store_strided(rows_ref, start + 1, series, 2, -second * scale)
        return carry

    lax.fori_loop(0, LATS, one_lat, 0)
    select = select_matrix(waves_ref[...], wave_count)
    rows = strided_rows(rows_ref, 0, rows_ref.shape[1], None).astype(jnp.bfloat16)
    moved[...] = jnp.dot(rows, select, preferred_element_type=jnp.float32)
    for group in range(moved.shape[1] // LANES):
        cut = pl.ds(group * LANES, LANES)
        for start in range(0, comps, 16):
            arrays = exchange(
                [moved[pl.ds(lat * comps + start, 16), cut] for lat in range(LATS)], 1
            )
            for place, value in enumerate(arrays):
                out_ref[group * LATS + place, pl.ds(start, 16), :] = value.astype(jnp.bfloat16)


def mix_weights(matrix_ref, row):
    pairs = {}
    for target in range(2):
        for source in range(2):
            for shift in range(4):
                value = jnp.zeros(row.shape, jnp.float32)
                for mode in range(4):
                    scalar = matrix_ref[target * 4 + mode, source * 4 + (mode - shift) % 4]
                    value = jnp.where(row // 2 == mode, scalar, value)
                pairs[target, source, shift] = value
    return pairs


def mix(weights_ref, which, tiles):
    shifted = [
        [tile if shift == 0 else pltpu.roll(tile, 2 * shift, 0) for shift in range(4)]
        for tile in tiles
    ]
    results = []
    for target in range(2):
        total = None
        for source in range(2):
            for shift in range(4):
                weight = weights_ref[which * 16 + target * 8 + source * 4 + shift]
                term = weight * shifted[source][shift]
                total = term if total is None else total + term
        results.append(total)
    return results


def spectral_kernel(
    slots, waves_ref, mode_in_ref, mode_out_ref, rates_ref, got_ref, legendre_ref,
    out_ref, energy_ref, rows_ref, weights_ref, factor_ref, packed_ref, back_ref, total_ref,
):
    devices, comps = got_ref.shape[0], got_ref.shape[1]
    wide = devices // 2
    wave_count = legendre_ref.shape[1]
    device = lax.axis_index("wide") * 2 + lax.axis_index("lev")
    row = lax.broadcasted_iota(jnp.int32, (8, LANES), 0)
    for which, matrix_ref in enumerate((mode_in_ref, mode_out_ref)):
        for (target, source, shift), value in mix_weights(matrix_ref, row).items():
            weights_ref[which * 16 + target * 8 + source * 4 + shift] = value
    degree = lax.broadcasted_iota(jnp.int32, (8, wave_count), 1).astype(jnp.float32)
    laplace = degree * (degree + 1.0) / (wave_count * wave_count)
    wide_row = lax.broadcasted_iota(jnp.int32, (8, wave_count), 0)
    for target in range(2):
        rate = jnp.zeros((8, wave_count), jnp.float32)
        for mode in range(4):
            rate = jnp.where(wide_row // 2 == mode, rates_ref[target * 4 + mode], rate)
        factor_ref[target] = 1.0 / (1.0 + 4.0 * laplace * rate)
        factor_ref[2 + target] = 2.0 * rate
    factor_ref[4] = 2.0 * laplace
    factor_ref[5] = 1.0 / (1.0 + 8.0 * laplace * laplace)
    factor_ref[6] = wave_count / (degree + 1.0)
    total_ref[...] = jnp.zeros_like(total_ref)

    for lev in range(2):
        for start in range(0, comps, 16):
            place = pl.ds(lev * comps + start, 16)
            for group in range(wide // PAD_SLOTS):
                arrays = exchange(
                    [
                        got_ref[(group * PAD_SLOTS + w) * 2 + lev, pl.ds(start, 16), :].astype(
                            jnp.float32
                        )
                        for w in range(PAD_SLOTS)
                    ],
                    LATS,
                )
                for slot in range(slots):
                    rows_ref[slot, place, pl.ds(group * LANES, LANES)] = arrays[slot].astype(
                        jnp.bfloat16
                    )

    def one_slot(slot, carry):
        spectral = lax.dot_general(
            rows_ref[slot], legendre_ref[slot], (((1,), (1,)), ((), ())),
            preferred_element_type=jnp.float32,
        )
        own_wave = waves_ref[device * slots + slot]
        for start in range(0, wave_count, LANES):
            cut = pl.ds(start, LANES)
            lane = lax.broadcasted_iota(jnp.int32, (8, LANES), 1) + start
            kept = lane >= own_wave

            def tile(lev, index):
                first = lev * comps + index * 8
                return jnp.where(kept, spectral[first : first + 8, start : start + LANES], 0.0)

            div_modes = mix(weights_ref, 0, [tile(lev, 0) for lev in range(2)])
            geo_modes = mix(weights_ref, 0, [tile(lev, 1) for lev in range(2)])
            twice = factor_ref[4, :, cut]
            div_next = [
                (div_modes[lev] + twice * geo_modes[lev]) * factor_ref[lev, :, cut]
                for lev in range(2)
            ]
            geo_next = [
                geo_modes[lev] - factor_ref[2 + lev, :, cut] * div_next[lev] for lev in range(2)
            ]
            div_level = mix(weights_ref, 1, div_next)
            geo_level = mix(weights_ref, 1, geo_next)
            damp = factor_ref[5, :, cut]
            for lev in range(2):
                total_ref[lev, :, cut] += div_level[lev] * div_level[lev]
                tiles = [div_level[lev], geo_level[lev]] + [
                    tile(lev, index) * damp for index in range(2, comps // 8)
                ]
                for index in range(0, comps // 8, 2):
                    packed_ref[pl.ds(lev * comps + index * 8, 16), cut] = jnp.concatenate(
                        tiles[index : index + 2], axis=0
                    ).astype(jnp.bfloat16)
        back_ref[slot] = jnp.dot(
            packed_ref[...], legendre_ref[slot], preferred_element_type=jnp.float32
        )
        return carry

    lax.fori_loop(0, slots, one_slot, 0)

    for lev in range(2):
        for start in range(0, comps, 16):
            place = pl.ds(lev * comps + start, 16)
            for group in range(wide // PAD_SLOTS):
                arrays = exchange(
                    [
                        back_ref[slot, place, pl.ds(group * LANES, LANES)]
                        if slot < slots
                        else jnp.zeros((16, LANES), jnp.float32)
                        for slot in range(PAD_SLOTS)
                    ],
                    LATS,
                )
                for w in range(PAD_SLOTS):
                    out_ref[(group * PAD_SLOTS + w) * 2 + lev, pl.ds(start, 16), :] = arrays[
                        w
                    ].astype(jnp.bfloat16)

    share = wave_count // devices
    for start in range(0, wave_count, LANES):
        cut = pl.ds(start, LANES)
        first, second = total_ref[0, :, cut], total_ref[1, :, cut]
        first = first + pltpu.roll(first, 7, 0)
        second = second + pltpu.roll(second, 1, 0)
        both = jnp.where(row % 2 == 0, first, second) * factor_ref[6, :, cut]
        for target in range(start // share, (start + LANES) // share):
            energy_ref[target] = both


def inverse_kernel(
    fields, wave_count, points_ref, waves_ref, got_ref, terms_ref, out_ref, energy_ref,
    cos_ref, sin_ref, base_ref, moved, rows_ref, values_ref,
):
    devices, comps = got_ref.shape[0], got_ref.shape[1]
    longitudes = out_ref.shape[1]
    series = comps // 2
    for group in range(devices // LATS):
        cut = pl.ds(group * LANES, LANES)
        for start in range(0, comps, 16):
            arrays = exchange(
                [
                    got_ref[group * LATS + place, pl.ds(start, 16), :].astype(jnp.float32)
                    for place in range(LATS)
                ],
                1,
            )
            for lat, value in enumerate(arrays):
                moved[pl.ds(lat * comps + start, 16), cut] = value.astype(jnp.bfloat16)
    select = select_matrix(waves_ref[...], wave_count)
    rows = lax.dot_general(
        moved[...], select, (((1,), (1,)), ((), ())), preferred_element_type=jnp.float32
    )
    for block in range(rows_ref.shape[0]):
        rows_ref[block] = rows[:, block * LANES : (block + 1) * LANES]
    position = lax.broadcasted_iota(jnp.int32, (series, longitudes), 1)
    wave = lax.broadcasted_iota(jnp.int32, (series, wave_count), 1)

    def one_lat(lat, carry):
        points = points_ref[lat]
        count = points.astype(jnp.float32)
        inverse = 1.0 / jnp.full((1, longitudes), count, jnp.float32)
        fill_tables(count, inverse, cos_ref, sin_ref, base_ref)
        factor = jnp.where(wave < (points + 1) // 2, jnp.where(wave == 0, 1.0, 2.0), 0.0)
        start = lat * comps
        first = (strided_rows(rows_ref, start, series, 2) * factor).astype(jnp.bfloat16)
        second = (strided_rows(rows_ref, start + 1, series, 2) * factor).astype(jnp.bfloat16)
        values = jnp.dot(first, cos_ref[...], preferred_element_type=jnp.float32) - jnp.dot(
            second, sin_ref[...], preferred_element_type=jnp.float32
        )
        values = jnp.where(position < points, values, 0.0)
        store_strided(values_ref, lat, series, LATS, values)
        return carry

    lax.fori_loop(0, LATS, one_lat, 0)
    tendency_out(values_ref, out_ref, fields)

    energy = terms_ref[0]
    for source in range(1, devices):
        energy = energy + terms_ref[source]
    share = wave_count // devices
    device = lax.axis_index("wide") * 2 + lax.axis_index("lev")
    energy = pltpu.roll(energy, lax.rem(LANES - lax.rem(device * share, LANES), LANES), 1)
    for lev in range(2):
        for level in range(4):
            energy_ref[lev * 4 + level : lev * 4 + level + 1, :] = energy[
                2 * level + lev : 2 * level + lev + 1, :share
            ]


def vmem():
    return pl.BlockSpec(memory_space=pltpu.VMEM)


def smem():
    return pl.BlockSpec(memory_space=pltpu.SMEM)


def body(
    model_state, grid_points, quad_weights, slot_waves, legendre, mode_in, mode_out, mode_rates
):
    fields, lev_local, lat_local, longitudes = model_state.shape
    slots, wave_count, lat_all = legendre.shape
    devices = lax.axis_size("wide") * lax.axis_size("lev")
    comps = 2 * fields * lev_local
    assert (lev_local, lat_local, lax.axis_size("lev")) == (4, LATS, 2)
    params = pltpu.CompilerParams(vmem_limit_bytes=VMEM)
    f32, bf16 = jnp.float32, jnp.bfloat16
    blocks = jax.ShapeDtypeStruct((devices, comps, LANES), bf16)
    terms = jax.ShapeDtypeStruct((devices, 8, LANES), f32)

    waves = slot_waves.reshape(devices // LATS, LATS, slots)
    waves = jnp.pad(waves, ((0, 0), (0, 0), (0, PAD_SLOTS - slots)), constant_values=-1)
    waves = jnp.transpose(waves, (0, 2, 1)).reshape(1, devices * PAD_SLOTS)
    places = waves.shape[1]

    sent = pl.pallas_call(
        partial(forward_kernel, fields, wave_count),
        out_shape=blocks,
        in_specs=[smem(), smem(), vmem(), vmem()],
        out_specs=vmem(),
        scratch_shapes=[
            pltpu.VMEM((longitudes // LANES, fields * lev_local * lat_local, LANES), f32),
            pltpu.VMEM((longitudes, wave_count), bf16),
            pltpu.VMEM((longitudes, wave_count), bf16),
            pltpu.VMEM((2, 16 + longitudes // 16, wave_count), f32),
            pltpu.VMEM((wave_count // LANES, lat_local * comps, LANES), f32),
            pltpu.VMEM((lat_local * comps, places), f32),
        ],
        compiler_params=params,
    )(grid_points, quad_weights, model_state.reshape(-1, longitudes), waves)
    got = lax.all_to_all(sent, ("wide", "lev"), split_axis=0, concat_axis=0, tiled=True)

    back, energy_terms = pl.pallas_call(
        partial(spectral_kernel, slots),
        out_shape=(blocks, terms),
        in_specs=[smem(), smem(), smem(), smem(), vmem(), vmem()],
        out_specs=(vmem(), vmem()),
        scratch_shapes=[
            pltpu.VMEM((slots, 2 * comps, lat_all), bf16),
            pltpu.VMEM((32, 8, LANES), f32),
            pltpu.VMEM((7, 8, wave_count), f32),
            pltpu.VMEM((2 * comps, wave_count), bf16),
            pltpu.VMEM((slots, 2 * comps, lat_all), f32),
            pltpu.VMEM((2, 8, wave_count), f32),
        ],
        compiler_params=params,
    )(slot_waves, mode_in, mode_out, mode_rates, got, legendre)
    arrived = lax.all_to_all(back, ("wide", "lev"), split_axis=0, concat_axis=0, tiled=True)
    parts = lax.all_to_all(energy_terms, ("wide", "lev"), split_axis=0, concat_axis=0, tiled=True)

    new_state, energy = pl.pallas_call(
        partial(inverse_kernel, fields, wave_count),
        out_shape=(
            jax.ShapeDtypeStruct((fields * lev_local * lat_local, longitudes), f32),
            jax.ShapeDtypeStruct((8, wave_count // devices), f32),
        ),
        in_specs=[smem(), vmem(), vmem(), vmem()],
        out_specs=(vmem(), vmem()),
        scratch_shapes=[
            pltpu.VMEM((wave_count, longitudes), bf16),
            pltpu.VMEM((wave_count, longitudes), bf16),
            pltpu.VMEM((2, 16 + wave_count // 16, longitudes), f32),
            pltpu.VMEM((lat_local * comps, places), bf16),
            pltpu.VMEM((wave_count // LANES, lat_local * comps, LANES), f32),
            pltpu.VMEM((longitudes // LANES, fields * lev_local * lat_local, LANES), f32),
        ],
        compiler_params=params,
    )(grid_points, waves, arrived, parts)
    return (new_state.reshape(model_state.shape), energy)


def solution(mesh):
    return jax.shard_map(
        body,
        mesh=mesh,
        in_specs=(
            P("ens", "lev", "wide", None),
            P("wide"),
            P("wide"),
            P(),
            P(("wide", "lev"), None, None),
            P(),
            P(),
            P(),
        ),
        out_specs=(P("ens", "lev", "wide", None), P("ens", ("wide", "lev"))),
        check_vma=False,
    )
```

time: 867 us -> 74.8 us (0.09)
  other arithmetic: 488 us -> 0 us
  waiting for transfers between devices: 144 us -> 0 us
  local copies, waits for them, and re-layouts: 132 us -> 7.58 us
  loops' own time: 48.5 us -> 0 us
  blocking collectives: 0 us -> 40.5 us
  Pallas kernels: 0 us -> 25.7 us
  matrix products: 22.4 us -> 0 us
  between operations: 14.8 us -> 0.67 us
  starting transfers between devices: 9.92 us -> 0 us
    another operation x19 -> x0, other arithmetic: 469 us -> none
    unnamed x2 -> x0, waiting for transfers between devices: 137 us -> none
    another operation x2 -> x0, loops' own time: 48.5 us -> none  [the longest x1 26.3 us: body(): lax.map(partial(forward_lat, longitudes, wave_count), (by_lat, grid_point...]
    all_to_all x0 -> x3, blocking collectives: none -> 40.5 us  [the longest x1 17.7 us: body(): lax.all_to_all(sent, ('wide', 'lev'), split_axis=0, concat_axis=0, tiled=...]
    gather x3 -> x0, local copies, waits for them, and re-layouts: 37.6 us -> none  [the longest x1 27.8 us: body(): ordered = jnp.take(fourier, slot_waves, axis=4)]
    pallas_call x0 -> x3, Pallas kernels: none -> 25.7 us  [the longest x1 9.3 us: body(): pl.pallas_call(partial(inverse_kernel, fields, wave_count), out_shape=(ja...]
    dot_general x22 -> x0, matrix products: 22.4 us -> none  [the longest x8 12.9 us: forward_lat(): fourier = jnp.dot(row_block, tables, preferred_element_type=jnp.float32)]
    unnamed x22 -> x18, local copies, waits for them, and re-layouts: 22.5 us -> 6.65 us
  transfers between devices with their start and end apart: 3 -> 0, of which waited for: 2 -> 0; matrix products, arithmetic and copies ran while one was open for 1% -> 0% of each run, Pallas kernels for 0% -> 0%
where the time goes in v1:
time: 74.8 us; the launch traced here: 74.4 us
  blocking collectives  40.5 us (54%)
  Pallas kernels  25.7 us (34%)
  local copies, waits for them, and re-layouts  7.58 us (10%)
    all_to_all x1, blocking collectives, body(): lax.all_to_all(sent, ('wide', 'lev'), split_axis=0, concat_axis=0, tiled=...  17.7 us
    all_to_all x1, blocking collectives, body(): lax.all_to_all(back, ('wide', 'lev'), split_axis=0, concat_axis=0, tiled=...  12.4 us
    all_to_all x1, blocking collectives, body(): lax.all_to_all(energy_terms, ('wide', 'lev'), split_axis=0, concat_axis=0...  10.4 us
    pallas_call x1, Pallas kernels, body(): pl.pallas_call(partial(inverse_kernel, fields, wave_count), out_shape=(ja...  9.3 us
    pallas_call x1, Pallas kernels, body(): pl.pallas_call(partial(spectral_kernel, slots), out_shape=(blocks, terms)...  8.31 us
    pallas_call x1, Pallas kernels, body(): pl.pallas_call(partial(forward_kernel, fields, wave_count), out_shape=blo...  8.06 us
    unnamed x18, local copies, waits for them, and re-layouts  6.65 us

profile of v1, /device:TPU:0, one launch (start us, length us, event | category | flops | bytes accessed | tf_op | source)
XLA Modules:
  0.0 74.4 jit_solution(8313029152479371098)
XLA Ops:
  0.6 0.8 %reshape.16 = s32[4,8,16]{2,1,0:T(8,128)S(1)} reshape(s32[512]{0:T(512)} %waves_ref.1) | data formatting | bytes 4096 | tf_op jit(solution)/shard_map/reshape | solution.py:383
  1.4 0.1 copy.10
  1.5 0.1 reshape.17.waves_ref
  1.6 0.0 copy-start.1
  1.6 1.0 %copy-done.1 = f32[4,4,8,1024]{3,2,1,0:T(8,128)S(1)} copy-done((f32[4,4,8,1024]{3,2,1,0:T(8,128)S(1)}, f32[4,4,8,1024]{3,2,1,0:T(8,128)}, u32[]{:S(2)}) %copy-start.1) | copy-done | bytes 524312
  2.6 0.0 copy-start.5
  2.6 0.7 copy-done.5
  3.3 0.0 copy-start.7
  3.3 0.7 copy-done.7
  3.9 0.0 copy-start.6
  3.9 8.1 %shard_map.95 = bf16[32,32,128]{2,1,0:T(8,128)(2,1)S(1)} custom-call(s32[8]{0:T(128)S(1)} %copy-done.5, f32[8]{0:T(128)S(1)} %copy-done.7, f32[128,1024]{1,0:T(8,128)S(1)} %bitcast.3, s32[1,512]{1,0:T(1,128)S(1)} %reshape.17.waves_ref), custom_call_target="tpu_custom_call" | custom-call | tf_op jit(solution)/shard_map/pallas_call | solution.py:388
  12.0 17.7 %all_to_all.15.got_ref = bf16[32,32,128]{2,1,0:T(8,128)(2,1)S(1)} all-to-all(bf16[32,32,128]{2,1,0:T(8,128)(2,1)S(1)} %shard_map.95), channel_id=1, replica_groups=mesh['ens'=1,'wide'=16,'lev'=2] {'wide','lev'}, dimensions={0} | all-to-all | bytes 524288 | tf_op jit(solution)/shard_map/all_to_all | solution.py:403
  29.7 0.0 copy-start
  29.7 1.6 %copy-done = bf16[16,512,128]{2,1,0:T(8,128)(2,1)S(1)} copy-done((bf16[16,512,128]{2,1,0:T(8,128)(2,1)S(1)}, bf16[16,512,128]{2,1,0:T(8,128)(2,1)}, u32[]{:S(2)}) %copy-start) | copy-done | bytes 2097176
  31.3 0.0 copy-start.2
  31.3 0.7 copy-done.2
  32.0 0.0 copy-start.3
  32.0 0.7 copy-done.3
  32.7 0.0 copy-start.4
  32.7 0.7 copy-done.4
  33.3 0.0 copy-start.8
  33.3 0.7 copy-done.8
  34.0 8.3 %shard_map.96 = (bf16[32,32,128]{2,1,0:T(8,128)(2,1)S(1)}, f32[32,8,128]{2,1,0:T(8,128)S(1)}) custom-call(s32[512]{0:T(512)S(1)} %copy-done.2, f32[8,8]{1,0:T(8,128)S(1)} %copy-done.3, f32[8,8]{1,0:T(8,128)S(1)} %copy-done.4, f32[8]{0:T(128)S(1)} %copy-done.8, bf16[32,32,128]{2,1,0:T(8,128)(2,1)S(1)} %all_to_all.15.got_ref, bf16[16,512,128]{2,1,0:T(8,128)(2,1)S(1)} %copy-done), custom_call_target="tpu_custom_call" | custom-call | tf_op jit(solution)/shard_map/pallas_call | solution.py:405
  42.3 10.4 %all_to_all.16.terms_ref = f32[32,8,128]{2,1,0:T(8,128)S(1)} all-to-all(f32[32,8,128]{2,1,0:T(8,128)S(1)} %get-tuple-element.7), channel_id=1, replica_groups=mesh['ens'=1,'wide'=16,'lev'=2] {'wide','lev'}, dimensions={0} | all-to-all | bytes 262144 | tf_op jit(solution)/shard_map/all_to_all | solution.py:421
  52.8 12.4 %all_to_all.17.got_ref = bf16[32,32,128]{2,1,0:T(8,128)(2,1)S(1)} all-to-all(bf16[32,32,128]{2,1,0:T(8,128)(2,1)S(1)} %get-tuple-element.6), channel_id=1, replica_groups=mesh['ens'=1,'wide'=16,'lev'=2] {'wide','lev'}, dimensions={0} | all-to-all | bytes 524288 | tf_op jit(solution)/shard_map/all_to_all | solution.py:420
  65.1 0.0 copy-done.6
  65.1 9.3 %shard_map.97 = (f32[128,1024]{1,0:T(8,128)}, f32[8,16]{1,0:T(8,128)}) custom-call(s32[8]{0:T(128)S(1)} %copy-done.6, s32[1,512]{1,0:T(1,128)S(1)} %reshape.17.waves_ref, bf16[32,32,128]{2,1,0:T(8,128)(2,1)S(1)} %all_to_all.17.got_ref, f32[32,8,128]{2,1,0:T(8,128)S(1)} %all_to_all.16.terms_ref), custom_call_target="tpu_custom_call" | custom-call | tf_op jit(solution)/shard_map/pallas_call | solution.py:423
Async XLA Ops:
  1.6 1.0 %copy-start.1 = (f32[4,4,8,1024]{3,2,1,0:T(8,128)S(1)}, f32[4,4,8,1024]{3,2,1,0:T(8,128)}, u32[]{:S(2)}) copy-start(f32[4,4,8,1024]{3,2,1,0:T(8,128)} %param.8) | copy-start | bytes 1572868
  2.6 0.7 copy-start.5
  3.3 0.7 copy-start.7
  3.9 61.2 %copy-start.6 = (s32[8]{0:T(128)S(1)}, s32[8]{0:T(128)}, u32[]{:S(2)}) copy-start(s32[8]{0:T(128)} %points_ref.3) | copy-start | bytes 100
  29.7 1.6 %copy-start = (bf16[16,512,128]{2,1,0:T(8,128)(2,1)S(1)}, bf16[16,512,128]{2,1,0:T(8,128)(2,1)}, u32[]{:S(2)}) copy-start(bf16[16,512,128]{2,1,0:T(8,128)(2,1)} %legendre_ref.1) | copy-start | bytes 6291460
  31.3 0.7 copy-start.2
  32.0 0.7 copy-start.3
  32.7 0.7 copy-start.4
  33.3 0.7 copy-start.8

commit v2 on v1

--- a/solution.py
+++ b/solution.py
@@ -367,6 +367,80 @@
     return pl.BlockSpec(memory_space=pltpu.SMEM)
 
 
+def swap_kernel(devices, count, *refs):
+    sources, targets = refs[:count], refs[count : 2 * count]
+    send_sem, recv_sem, own_sem = refs[2 * count :]
+    me = lax.axis_index("wide") * 2 + lax.axis_index("lev")
+
+    def place(peer):
+        return {"wide": peer // 2, "lev": lax.rem(peer, 2)}
+
+    barrier = pltpu.get_barrier_semaphore()
+
+    def greet(offset, carry):
+        peer = lax.rem(me + offset, devices)
+        pl.semaphore_signal(
+            barrier, inc=1, device_id=place(peer), device_id_type=pl.DeviceIdType.MESH
+        )
+        return carry
+
+    lax.fori_loop(1, devices, greet, 0)
+    own = [
+        pltpu.make_async_copy(sources[k].at[me], targets[k].at[me], own_sem.at[k])
+        for k in range(count)
+    ]
+    for copy in own:
+        copy.start()
+    pl.semaphore_wait(barrier, devices - 1)
+
+    def copies(offset):
+        peer = lax.rem(me + offset, devices)
+        return [
+            pltpu.make_async_remote_copy(
+                src_ref=sources[k].at[peer],
+                dst_ref=targets[k].at[me],
+                send_sem=send_sem.at[k, offset],
+                recv_sem=recv_sem.at[k, offset],
+                device_id=place(peer),
+                device_id_type=pl.DeviceIdType.MESH,
+            )
+            for k in range(count)
+        ]
+
+    def send(offset, carry):
+        for copy in copies(offset):
+            copy.start()
+        return carry
+
+    def finish(offset, carry):
+        for copy in copies(offset):
+            copy.wait()
+        return carry
+
+    lax.fori_loop(1, devices, send, 0)
+    lax.fori_loop(1, devices, finish, 0)
+    for copy in own:
+        copy.wait()
+
+
+def swap(arrays, devices, collective):
+    count = len(arrays)
+    return pl.pallas_call(
+        partial(swap_kernel, devices, count),
+        out_shape=tuple(jax.ShapeDtypeStruct(a.shape, a.dtype) for a in arrays),
+        in_specs=[vmem()] * count,
+        out_specs=(vmem(),) * count,
+        scratch_shapes=[
+            pltpu.SemaphoreType.DMA((count, devices)),
+            pltpu.SemaphoreType.DMA((count, devices)),
+            pltpu.SemaphoreType.DMA((count,)),
+        ],
+        compiler_params=pltpu.CompilerParams(
+            vmem_limit_bytes=VMEM, collective_id=collective, has_side_effects=True
+        ),
+    )(*arrays)
+
+
 def body(
     model_state, grid_points, quad_weights, slot_waves, legendre, mode_in, mode_out, mode_rates
 ):
@@ -400,7 +474,7 @@
         ],
         compiler_params=params,
     )(grid_points, quad_weights, model_state.reshape(-1, longitudes), waves)
-    got = lax.all_to_all(sent, ("wide", "lev"), split_axis=0, concat_axis=0, tiled=True)
+    (got,) = swap([sent], devices, 0)
 
     back, energy_terms = pl.pallas_call(
         partial(spectral_kernel, slots),
@@ -417,8 +491,7 @@
         ],
         compiler_params=params,
     )(slot_waves, mode_in, mode_out, mode_rates, got, legendre)
-    arrived = lax.all_to_all(back, ("wide", "lev"), split_axis=0, concat_axis=0, tiled=True)
-    parts = lax.all_to_all(energy_terms, ("wide", "lev"), split_axis=0, concat_axis=0, tiled=True)
+    arrived, parts = swap([back, energy_terms], devices, 1)
 
     new_state, energy = pl.pallas_call(
         partial(inverse_kernel, fields, wave_count),

time: 74.8 us -> 62.5 us (0.84)
  the two profiles are of different devices: /device:TPU:0 before, /device:TPU:15 now
where the time goes in v2:
time: 62.5 us; the launch traced here: 62.2 us
  Pallas kernels  53.9 us (86%)
  local copies, waits for them, and re-layouts  7.58 us (12%)
  between operations  0.7 us (1%)
    pallas_call x2, Pallas kernels, swap(): pl.pallas_call(partial(swap_kernel, devices, count), out_shape=tuple((jax...  28.2 us
    pallas_call x1, Pallas kernels, body(): pl.pallas_call(partial(inverse_kernel, fields, wave_count), out_shape=(ja...  9.31 us
    pallas_call x1, Pallas kernels, body(): pl.pallas_call(partial(spectral_kernel, slots), out_shape=(blocks, terms)...  8.3 us
    pallas_call x1, Pallas kernels, body(): pl.pallas_call(partial(forward_kernel, fields, wave_count), out_shape=blo...  8.06 us
    unnamed x18, local copies, waits for them, and re-layouts  6.65 us

profile of v2, /device:TPU:15, one launch (start us, length us, event | category | flops | bytes accessed | tf_op | source)
XLA Modules:
  0.0 62.2 jit_solution(11071655905937430109)
XLA Ops:
  0.6 0.0 copy-start.6
  0.6 0.8 %reshape.16 = s32[4,8,16]{2,1,0:T(8,128)S(1)} reshape(s32[512]{0:T(512)} %waves_ref.1) | data formatting | bytes 4096 | tf_op jit(solution)/shard_map/reshape | solution.py:457
  1.4 0.1 copy.10
  1.5 0.1 reshape.17.waves_ref
  1.6 0.0 copy-start.1
  1.6 1.0 %copy-done.1 = f32[4,4,8,1024]{3,2,1,0:T(8,128)S(1)} copy-done((f32[4,4,8,1024]{3,2,1,0:T(8,128)S(1)}, f32[4,4,8,1024]{3,2,1,0:T(8,128)}, u32[]{:S(2)}) %copy-start.1) | copy-done | bytes 524312
  2.6 0.0 copy-start.5
  2.6 0.7 %copy-done.5 = s32[8]{0:T(128)S(1)} copy-done((s32[8]{0:T(128)S(1)}, s32[8]{0:T(128)}, u32[]{:S(2)}) %copy-start.5) | copy-done | bytes 56
  3.3 0.0 copy-start.7
  3.3 0.7 %copy-done.7 = f32[8]{0:T(128)S(1)} copy-done((f32[8]{0:T(128)S(1)}, f32[8]{0:T(128)}, u32[]{:S(2)}) %copy-start.7) | copy-done | bytes 56
  3.9 8.1 %shard_map.95.refs_0_ = bf16[32,32,128]{2,1,0:T(8,128)(2,1)S(1)} custom-call(s32[8]{0:T(128)S(1)} %copy-done.5, f32[8]{0:T(128)S(1)} %copy-done.7, f32[128,1024]{1,0:T(8,128)S(1)} %bitcast.3, s32[1,512]{1,0:T(1,128)S(1)} %reshape.17.waves_ref), custom_call_target="tpu_custom_call" | custom-call | tf_op jit(solution)/shard_map/pallas_call | solution.py:462
  12.0 12.7 %shard_map.96.got_ref = bf16[32,32,128]{2,1,0:T(8,128)(2,1)S(1)} custom-call(bf16[32,32,128]{2,1,0:T(8,128)(2,1)S(1)} %shard_map.95.refs_0_), custom_call_target="tpu_custom_call" | custom-call | tf_op jit(solution)/shard_map/pallas_call | solution.py:428
  24.7 0.0 copy-start
  24.8 1.6 %copy-done = bf16[16,512,128]{2,1,0:T(8,128)(2,1)S(1)} copy-done((bf16[16,512,128]{2,1,0:T(8,128)(2,1)S(1)}, bf16[16,512,128]{2,1,0:T(8,128)(2,1)}, u32[]{:S(2)}) %copy-start) | copy-done | bytes 2097176
  26.3 0.0 copy-start.2
  26.3 0.7 %copy-done.2 = s32[512]{0:T(512)S(1)} copy-done((s32[512]{0:T(512)S(1)}, s32[512]{0:T(512)}, u32[]{:S(2)}) %copy-start.2) | copy-done | bytes 2072
  27.0 0.0 copy-start.3
  27.0 0.7 %copy-done.3 = f32[8,8]{1,0:T(8,128)S(1)} copy-done((f32[8,8]{1,0:T(8,128)S(1)}, f32[8,8]{1,0:T(8,128)}, u32[]{:S(2)}) %copy-start.3) | copy-done | bytes 280
  27.7 0.0 copy-start.4
  27.7 0.7 %copy-done.4 = f32[8,8]{1,0:T(8,128)S(1)} copy-done((f32[8,8]{1,0:T(8,128)S(1)}, f32[8,8]{1,0:T(8,128)}, u32[]{:S(2)}) %copy-start.4) | copy-done | bytes 280
  28.4 0.0 copy-start.8
  28.4 0.7 %copy-done.8 = f32[8]{0:T(128)S(1)} copy-done((f32[8]{0:T(128)S(1)}, f32[8]{0:T(128)}, u32[]{:S(2)}) %copy-start.8) | copy-done | bytes 56
  29.1 8.3 %shard_map.97 = (bf16[32,32,128]{2,1,0:T(8,128)(2,1)S(1)}, f32[32,8,128]{2,1,0:T(8,128)S(1)}) custom-call(s32[512]{0:T(512)S(1)} %copy-done.2, f32[8,8]{1,0:T(8,128)S(1)} %copy-done.3, f32[8,8]{1,0:T(8,128)S(1)} %copy-done.4, f32[8]{0:T(128)S(1)} %copy-done.8, bf16[32,32,128]{2,1,0:T(8,128)(2,1)S(1)} %shard_map.96.got_ref, bf16[16,512,128]{2,1,0:T(8,128)(2,1)S(1)} %copy-done), custom_call_target="tpu_custom_call" | custom-call | tf_op jit(solution)/shard_map/pallas_call | solution.py:479
  37.4 15.5 %shard_map.98 = (bf16[32,32,128]{2,1,0:T(8,128)(2,1)S(1)}, f32[32,8,128]{2,1,0:T(8,128)S(1)}) custom-call(bf16[32,32,128]{2,1,0:T(8,128)(2,1)S(1)} %get-tuple-element.8.refs_0_, f32[32,8,128]{2,1,0:T(8,128)S(1)} %get-tuple-element.9.refs_1_), custom_call_target="tpu_custom_call" | custom-call | tf_op jit(solution)/shard_map/pallas_call | solution.py:428
  52.9 0.0 copy-done.6
  52.9 9.3 %shard_map.99 = (f32[128,1024]{1,0:T(8,128)}, f32[8,16]{1,0:T(8,128)}) custom-call(s32[8]{0:T(128)S(1)} %copy-done.6, s32[1,512]{1,0:T(1,128)S(1)} %reshape.17.waves_ref, bf16[32,32,128]{2,1,0:T(8,128)(2,1)S(1)} %get-tuple-element.10.got_ref, f32[32,8,128]{2,1,0:T(8,128)S(1)} %get-tuple-element.11.terms_ref), custom_call_target="tpu_custom_call" | custom-call | tf_op jit(solution)/shard_map/pallas_call | solution.py:496
Async XLA Ops:
  0.6 52.3 %copy-start.6 = (s32[8]{0:T(128)S(1)}, s32[8]{0:T(128)}, u32[]{:S(2)}) copy-start(s32[8]{0:T(128)} %points_ref.3) | copy-start | bytes 100
  1.6 1.0 %copy-start.1 = (f32[4,4,8,1024]{3,2,1,0:T(8,128)S(1)}, f32[4,4,8,1024]{3,2,1,0:T(8,128)}, u32[]{:S(2)}) copy-start(f32[4,4,8,1024]{3,2,1,0:T(8,128)} %param.8) | copy-start | bytes 1572868
  2.6 0.7 %copy-start.5 = (s32[8]{0:T(128)S(1)}, s32[8]{0:T(128)}, u32[]{:S(2)}) copy-start(s32[8]{0:T(128)} %points_ref.3) | copy-start | bytes 100
  3.3 0.7 %copy-start.7 = (f32[8]{0:T(128)S(1)}, f32[8]{0:T(128)}, u32[]{:S(2)}) copy-start(f32[8]{0:T(128)} %weight_ref.1) | copy-start | bytes 100
  24.7 1.6 %copy-start = (bf16[16,512,128]{2,1,0:T(8,128)(2,1)S(1)}, bf16[16,512,128]{2,1,0:T(8,128)(2,1)}, u32[]{:S(2)}) copy-start(bf16[16,512,128]{2,1,0:T(8,128)(2,1)} %legendre_ref.1) | copy-start | bytes 6291460
  26.3 0.7 %copy-start.2 = (s32[512]{0:T(512)S(1)}, s32[512]{0:T(512)}, u32[]{:S(2)}) copy-start(s32[512]{0:T(512)} %waves_ref.1) | copy-start | bytes 6148
  27.0 0.7 %copy-start.3 = (f32[8,8]{1,0:T(8,128)S(1)}, f32[8,8]{1,0:T(8,128)}, u32[]{:S(2)}) copy-start(f32[8,8]{1,0:T(8,128)} %mode_in_ref.1) | copy-start | bytes 772
  27.7 0.7 %copy-start.4 = (f32[8,8]{1,0:T(8,128)S(1)}, f32[8,8]{1,0:T(8,128)}, u32[]{:S(2)}) copy-start(f32[8,8]{1,0:T(8,128)} %mode_out_ref.1) | copy-start | bytes 772
  28.4 0.7 %copy-start.8 = (f32[8]{0:T(128)S(1)}, f32[8]{0:T(128)}, u32[]{:S(2)}) copy-start(f32[8]{0:T(128)} %rates_ref.1) | copy-start | bytes 100

commit v3 on v2

--- a/solution.py
+++ b/solution.py
@@ -183,9 +183,22 @@
 
 
 def spectral_kernel(
-    slots, waves_ref, mode_in_ref, mode_out_ref, rates_ref, got_ref, legendre_ref,
+    slots, waves_src, mode_in_src, mode_out_src, rates_src, got_ref, legendre_src,
     out_ref, energy_ref, rows_ref, weights_ref, factor_ref, packed_ref, back_ref, total_ref,
+    waves_ref, mode_in_ref, mode_out_ref, rates_ref, legendre_ref, sems,
 ):
+    pairs = (
+        (mode_in_src, mode_in_ref), (mode_out_src, mode_out_ref), (rates_src, rates_ref),
+        (waves_src, waves_ref), (legendre_src, legendre_ref),
+    )
+    loads = [
+        pltpu.make_async_copy(source, target, sems.at[k])
+        for k, (source, target) in enumerate(pairs)
+    ]
+    for load in loads:
+        load.start()
+    for load in loads[:4]:
+        load.wait()
     devices, comps = got_ref.shape[0], got_ref.shape[1]
     wide = devices // 2
     wave_count = legendre_ref.shape[1]
@@ -225,6 +238,8 @@
                     rows_ref[slot, place, pl.ds(group * LANES, LANES)] = arrays[slot].astype(
                         jnp.bfloat16
                     )
+
+    loads[4].wait()
 
     def one_slot(slot, carry):
         spectral = lax.dot_general(
@@ -363,6 +378,10 @@
     return pl.BlockSpec(memory_space=pltpu.VMEM)
 
 
+def anywhere():
+    return pl.BlockSpec(memory_space=pl.ANY)
+
+
 def smem():
     return pl.BlockSpec(memory_space=pltpu.SMEM)
 
@@ -479,7 +498,7 @@
     back, energy_terms = pl.pallas_call(
         partial(spectral_kernel, slots),
         out_shape=(blocks, terms),
-        in_specs=[smem(), smem(), smem(), smem(), vmem(), vmem()],
+        in_specs=[anywhere()] * 4 + [vmem(), anywhere()],
         out_specs=(vmem(), vmem()),
         scratch_shapes=[
             pltpu.VMEM((slots, 2 * comps, lat_all), bf16),
@@ -488,6 +507,12 @@
             pltpu.VMEM((2 * comps, wave_count), bf16),
             pltpu.VMEM((slots, 2 * comps, lat_all), f32),
             pltpu.VMEM((2, 8, wave_count), f32),
+            pltpu.SMEM(slot_waves.shape, jnp.int32),
+            pltpu.SMEM(mode_in.shape, f32),
+            pltpu.SMEM(mode_out.shape, f32),
+            pltpu.SMEM(mode_rates.shape, f32),
+            pltpu.VMEM(legendre.shape, bf16),
+            pltpu.SemaphoreType.DMA((5,)),
         ],
         compiler_params=params,
     )(slot_waves, mode_in, mode_out, mode_rates, got, legendre)

time: 62.5 us -> 62.5 us (level)
  no operation moved by 1% of the time
where the time goes in v3:
time: 62.5 us; the launch traced here: 62.2 us
  Pallas kernels  53.9 us (86%)
  local copies, waits for them, and re-layouts  7.58 us (12%)
  between operations  0.7 us (1%)
    pallas_call x2, Pallas kernels, swap(): pl.pallas_call(partial(swap_kernel, devices, count), out_shape=tuple((jax...  28.2 us
    pallas_call x1, Pallas kernels, body(): pl.pallas_call(partial(inverse_kernel, fields, wave_count), out_shape=(ja...  9.31 us
    pallas_call x1, Pallas kernels, body(): pl.pallas_call(partial(spectral_kernel, slots), out_shape=(blocks, terms)...  8.28 us
    pallas_call x1, Pallas kernels, body(): pl.pallas_call(partial(forward_kernel, fields, wave_count), out_shape=blo...  8.06 us
    unnamed x18, local copies, waits for them, and re-layouts  6.65 us

profile of v3, /device:TPU:15, one launch (start us, length us, event | category | flops | bytes accessed | tf_op | source)
XLA Modules:
  0.0 62.2 jit_solution(13384043586571883021)
XLA Ops:
  0.6 0.0 copy-start.6
  0.6 0.8 %reshape.16 = s32[4,8,16]{2,1,0:T(8,128)S(1)} reshape(s32[512]{0:T(512)} %waves_src.1) | data formatting | bytes 4096 | tf_op jit(solution)/shard_map/reshape | solution.py:476
  1.4 0.1 copy.10
  1.5 0.1 reshape.17.waves_ref
  1.6 0.0 copy-start.1
  1.6 1.0 %copy-done.1 = f32[4,4,8,1024]{3,2,1,0:T(8,128)S(1)} copy-done((f32[4,4,8,1024]{3,2,1,0:T(8,128)S(1)}, f32[4,4,8,1024]{3,2,1,0:T(8,128)}, u32[]{:S(2)}) %copy-start.1) | copy-done | bytes 524312
  2.6 0.0 copy-start.5
  2.6 0.7 %copy-done.5 = s32[8]{0:T(128)S(1)} copy-done((s32[8]{0:T(128)S(1)}, s32[8]{0:T(128)}, u32[]{:S(2)}) %copy-start.5) | copy-done | bytes 56
  3.3 0.0 copy-start.7
  3.3 0.7 %copy-done.7 = f32[8]{0:T(128)S(1)} copy-done((f32[8]{0:T(128)S(1)}, f32[8]{0:T(128)}, u32[]{:S(2)}) %copy-start.7) | copy-done | bytes 56
  3.9 8.1 %shard_map.95.refs_0_ = bf16[32,32,128]{2,1,0:T(8,128)(2,1)S(1)} custom-call(s32[8]{0:T(128)S(1)} %copy-done.5, f32[8]{0:T(128)S(1)} %copy-done.7, f32[128,1024]{1,0:T(8,128)S(1)} %bitcast.3, s32[1,512]{1,0:T(1,128)S(1)} %reshape.17.waves_ref), custom_call_target="tpu_custom_call" | custom-call | tf_op jit(solution)/shard_map/pallas_call | solution.py:481
  12.0 12.7 %shard_map.96.got_ref = bf16[32,32,128]{2,1,0:T(8,128)(2,1)S(1)} custom-call(bf16[32,32,128]{2,1,0:T(8,128)(2,1)S(1)} %shard_map.95.refs_0_), custom_call_target="tpu_custom_call" | custom-call | tf_op jit(solution)/shard_map/pallas_call | solution.py:447
  24.7 0.0 copy-start
  24.8 1.6 %copy-done = bf16[16,512,128]{2,1,0:T(8,128)(2,1)S(1)} copy-done((bf16[16,512,128]{2,1,0:T(8,128)(2,1)S(1)}, bf16[16,512,128]{2,1,0:T(8,128)(2,1)}, u32[]{:S(2)}) %copy-start) | copy-done | bytes 2097176
  26.3 0.0 copy-start.2
  26.3 0.7 %copy-done.2 = s32[512]{0:T(512)S(1)} copy-done((s32[512]{0:T(512)S(1)}, s32[512]{0:T(512)}, u32[]{:S(2)}) %copy-start.2) | copy-done | bytes 2072
  27.0 0.0 copy-start.3
  27.0 0.7 %copy-done.3 = f32[8,8]{1,0:T(8,128)S(1)} copy-done((f32[8,8]{1,0:T(8,128)S(1)}, f32[8,8]{1,0:T(8,128)}, u32[]{:S(2)}) %copy-start.3) | copy-done | bytes 280
  27.7 0.0 copy-start.4
  27.7 0.7 %copy-done.4 = f32[8,8]{1,0:T(8,128)S(1)} copy-done((f32[8,8]{1,0:T(8,128)S(1)}, f32[8,8]{1,0:T(8,128)}, u32[]{:S(2)}) %copy-start.4) | copy-done | bytes 280
  28.4 0.0 copy-start.8
  28.4 0.7 %copy-done.8 = f32[8]{0:T(128)S(1)} copy-done((f32[8]{0:T(128)S(1)}, f32[8]{0:T(128)}, u32[]{:S(2)}) %copy-start.8) | copy-done | bytes 56
  29.1 8.3 %shard_map.97 = (bf16[32,32,128]{2,1,0:T(8,128)(2,1)S(1)}, f32[32,8,128]{2,1,0:T(8,128)S(1)}) custom-call(s32[512]{0:T(512)S(1)} %copy-done.2, f32[8,8]{1,0:T(8,128)S(1)} %copy-done.3, f32[8,8]{1,0:T(8,128)S(1)} %copy-done.4, f32[8]{0:T(128)S(1)} %copy-done.8, bf16[32,32,128]{2,1,0:T(8,128)(2,1)S(1)} %shard_map.96.got_ref, bf16[16,512,128]{2,1,0:T(8,128)(2,1)S(1)} %copy-done), custom_call_target="tpu_custom_call" | custom-call | tf_op jit(solution)/shard_map/pallas_call | solution.py:498
  37.3 15.5 %shard_map.98 = (bf16[32,32,128]{2,1,0:T(8,128)(2,1)S(1)}, f32[32,8,128]{2,1,0:T(8,128)S(1)}) custom-call(bf16[32,32,128]{2,1,0:T(8,128)(2,1)S(1)} %get-tuple-element.8.refs_0_, f32[32,8,128]{2,1,0:T(8,128)S(1)} %get-tuple-element.9.refs_1_), custom_call_target="tpu_custom_call" | custom-call | tf_op jit(solution)/shard_map/pallas_call | solution.py:447
  52.9 0.0 copy-done.6
  52.9 9.3 %shard_map.99 = (f32[128,1024]{1,0:T(8,128)}, f32[8,16]{1,0:T(8,128)}) custom-call(s32[8]{0:T(128)S(1)} %copy-done.6, s32[1,512]{1,0:T(1,128)S(1)} %reshape.17.waves_ref, bf16[32,32,128]{2,1,0:T(8,128)(2,1)S(1)} %get-tuple-element.10.got_ref, f32[32,8,128]{2,1,0:T(8,128)S(1)} %get-tuple-element.11.terms_ref), custom_call_target="tpu_custom_call" | custom-call | tf_op jit(solution)/shard_map/pallas_call | solution.py:521
Async XLA Ops:
  0.6 52.2 %copy-start.6 = (s32[8]{0:T(128)S(1)}, s32[8]{0:T(128)}, u32[]{:S(2)}) copy-start(s32[8]{0:T(128)} %points_ref.3) | copy-start | bytes 100
  1.6 1.0 %copy-start.1 = (f32[4,4,8,1024]{3,2,1,0:T(8,128)S(1)}, f32[4,4,8,1024]{3,2,1,0:T(8,128)}, u32[]{:S(2)}) copy-start(f32[4,4,8,1024]{3,2,1,0:T(8,128)} %param.8) | copy-start | bytes 1572868
  2.6 0.7 %copy-start.5 = (s32[8]{0:T(128)S(1)}, s32[8]{0:T(128)}, u32[]{:S(2)}) copy-start(s32[8]{0:T(128)} %points_ref.3) | copy-start | bytes 100
  3.3 0.7 %copy-start.7 = (f32[8]{0:T(128)S(1)}, f32[8]{0:T(128)}, u32[]{:S(2)}) copy-start(f32[8]{0:T(128)} %weight_ref.1) | copy-start | bytes 100
  24.7 1.6 %copy-start = (bf16[16,512,128]{2,1,0:T(8,128)(2,1)S(1)}, bf16[16,512,128]{2,1,0:T(8,128)(2,1)}, u32[]{:S(2)}) copy-start(bf16[16,512,128]{2,1,0:T(8,128)(2,1)} %legendre_src.1) | copy-start | bytes 6291460
  26.3 0.7 %copy-start.2 = (s32[512]{0:T(512)S(1)}, s32[512]{0:T(512)}, u32[]{:S(2)}) copy-start(s32[512]{0:T(512)} %waves_src.1) | copy-start | bytes 6148
  27.0 0.7 %copy-start.3 = (f32[8,8]{1,0:T(8,128)S(1)}, f32[8,8]{1,0:T(8,128)}, u32[]{:S(2)}) copy-start(f32[8,8]{1,0:T(8,128)} %mode_in_src.1) | copy-start | bytes 772
  27.7 0.7 %copy-start.4 = (f32[8,8]{1,0:T(8,128)S(1)}, f32[8,8]{1,0:T(8,128)}, u32[]{:S(2)}) copy-start(f32[8,8]{1,0:T(8,128)} %mode_out_src.1) | copy-start | bytes 772
  28.4 0.7 %copy-start.8 = (f32[8]{0:T(128)S(1)}, f32[8]{0:T(128)}, u32[]{:S(2)}) copy-start(f32[8]{0:T(128)} %rates_src.1) | copy-start | bytes 100
